TPU v7x, 1024 devices: a whole 4x8x16 slice. The times are simulated.
1024 devices in a mesh: group: 16 (over x_lo, y), tensor: 64 (over z, x_hi, core).
Axes of the slice: x: 4 (x_hi: 2, x_lo: 2; x = x_hi * 2 + x_lo), y: 8, z: 16, core: 2. Of those that a mesh axis runs over, the one named last changes fastest.
Arguments:
- hidden: bfloat16 [16, 1536, 5120], P('group', 'tensor'), may hold values from -120 to 120
- norm_gain: float32 [5120], replicated, may hold values from 0.5 to 1.5
- cotangent: bfloat16 [2048, 1536], P('tensor'), may hold values from -0.15625 to 0.15625
- master: float32 [2048, 5120], P(('tensor', 'group')), may hold values from -0.078125 to 0.078125
- first_moment: float32 [2048, 5120], P(('tensor', 'group')), may hold values from -1.2 to 1.2
- second_moment: float32 [2048, 5120], P(('tensor', 'group')), may hold values from 0.02 to 0.2
- old_cache: bfloat16 [16, 2048, 1536], P('group', 'tensor'), may hold values from -6 to 6
- stale_pages: int32 [16, 96], P('group'), may hold values 0 or 1
Outputs:
- new_master: float32 [2048, 5120], P(('tensor', 'group'))
- new_first: float32 [2048, 5120], P(('tensor', 'group'))
- new_second: float32 [2048, 5120], P(('tensor', 'group'))
- cache: bfloat16 [16, 2048, 1536], P('group', 'tensor')
Inputs may be any that keep to these rules, and one draw needn't show every extreme that they name: `stale_pages`: 1 marks a page of 16 rows whose keys and values are recomputed.
All inputs are finite; a program needn't handle non-finite values. No bound on the sum of `stale_pages` on one device may be relied on, other than what follows from the above.
Results may differ from a plain program's by a relative error of at most 0.0045.
Values may be sent and summed in bfloat16 or wider, within the bound.
A program may use at most 64 MiB of HBM per device.

v0:
```python
import jax
import jax.numpy as jnp
from jax import lax
from jax.sharding import PartitionSpec as P

PAGE = 16


learning_rate = 0.003
first_decay = 0.9
second_decay = 0.999
adam_epsilon = 1e-08
norm_epsilon = 1e-06
first_correction = 1.0
second_correction = 0.632304575229


def broadcast(value, axis, source):
    kept = jnp.where(lax.axis_index(axis) == source, value, 0).astype(value.dtype)
    return lax.psum(kept, axis)


def norm_rows(rows_in, norm_gain):
    values = rows_in.astype(jnp.float32)
    inverse = lax.rsqrt(jnp.mean(values * values, axis=-1, keepdims=True) + norm_epsilon)
    return (values * inverse * norm_gain).astype(jnp.bfloat16)


def adam_update(master, first_moment, second_moment, gradient):
    new_first = first_decay * first_moment + (1.0 - first_decay) * gradient
    new_second = second_decay * second_moment + (1.0 - second_decay) * gradient * gradient
    update_step = (
        new_first / first_correction / (jnp.sqrt(new_second / second_correction) + adam_epsilon)
    )
    return (master - learning_rate * update_step, new_first, new_second)


def project(weights, normed_rows):
    return lax.dot_general(
        weights, normed_rows, (((1,), (1,)), ((), ())), preferred_element_type=jnp.float32
    )


def local(
    hidden, norm_gain, cotangent, master, first_moment, second_moment, old_cache, stale_pages
):
    normed_local = norm_rows(hidden[0], norm_gain)
    own_rows = master.shape[0]
    group_index = lax.axis_index("group")
    normed_all = lax.all_gather(normed_local, "tensor", axis=0, tiled=True)
    gradient = jnp.dot(cotangent, normed_all, preferred_element_type=jnp.float32)
    learner_grad = broadcast(gradient.astype(jnp.bfloat16), "group", 0).astype(gradient.dtype)
    owned_grad = lax.dynamic_slice_in_dim(learner_grad, group_index * own_rows, own_rows, 0)
    new_master, new_first, new_second = adam_update(master, first_moment, second_moment, owned_grad)
    weights = lax.all_gather(new_master.astype(jnp.bfloat16), "group", axis=0, tiled=True)
    recomputed = project(weights, normed_all)
    page_mask = jnp.repeat(stale_pages[0], PAGE)
    cache = jnp.where(page_mask[None, :] > 0, recomputed.astype(jnp.bfloat16), old_cache[0])
    return (new_master, new_first, new_second, cache[None])


def solution(mesh):
    placed = (
        P("group", "tensor", None),
        P(),
        P("tensor", None),
        P(("tensor", "group"), None),
        P(("tensor", "group"), None),
        P(("tensor", "group"), None),
        P("group", "tensor", None),
        P("group", None),
    )
    return jax.shard_map(
        local,
        mesh=mesh,
        in_specs=placed,
        out_specs=(
            P(("tensor", "group"), None),
            P(("tensor", "group"), None),
            P(("tensor", "group"), None),
            P("group", "tensor", None),
        ),
        check_vma=False,
    )
```

profile of v0, /device:TPU:6, one launch (start us, length us, event | category | flops | bytes accessed | tf_op | source)
XLA Modules:
  0.0 423.4 jit_solution(7199966836294234024)
XLA Ops:
  7.2 0.0 copy-start
  7.2 0.0 copy-start.5
  7.2 0.0 copy-start.2
  7.2 0.0 copy-start.3
  7.2 0.0 copy-start.4
  7.2 0.0 copy-start.1
  7.2 0.0 all-gather.3.cloned.1.call-start
  7.3 1.2 fusion.4
  8.4 1.8 fusion.6
  10.2 0.0 all-gather.3.cloned.1.call-update
  10.2 0.0 all-reduce.2.cloned.1.call-start
  10.3 206.9 %all-gather.3.cloned.1.call-done = bf16[1536,5120]{1,0:T(8,128)(2,1)} async-done(((bf16[24,5120]{1,0:T(8,128)(2,1)}), bf16[1536,5120]{1,0:T(8,128)(2,1)}) %all-gather.3.cloned.1.call-update) | async-done | bytes 15728656 | tf_op jit(solution)/shard_map/all_gather | solution.py:50
  217.2 0.0 copy-done
  217.2 9.0 %fusion.1 = bf16[32,5120]{1,0:T(8,128)(2,1)} fusion(bf16[32,1536]{1,0:T(8,128)(2,1)S(1)} %copy-done, bf16[1536,5120]{1,0:T(8,128)(2,1)} %all-gather.3.cloned.1.call-done, pred[]{:T(512)S(6)} %eq.3), kind=kOutput, calls=%fused_computation.2 | convolution fusion | flops 503644160 | bytes 16154625 | tf_op jit(solution)/shard_map/dot_general | solution.py:51
  226.2 0.0 all-reduce.2.cloned.1.call-update
  226.2 0.1 broadcast_in_dim.21
  226.3 0.1 gt.21
  226.4 144.7 %all-reduce.2.cloned.1.call-done = bf16[32,5120]{1,0:T(8,128)(2,1)} async-done(((bf16[32,5120]{1,0:T(8,128)(2,1)}), bf16[32,5120]{1,0:T(8,128)(2,1)}) %all-reduce.2.cloned.1.call-update) | async-done | bytes 327696 | tf_op jit(solution)/shard_map/psum | solution.py:20
  371.2 0.0 copy-done.2
  371.2 0.0 copy-done.4
  371.2 1.7 convert_bitcast_fusion
  372.8 32.7 %all-gather = bf16[16,2,5120]{2,1,0:T(2,128)(2,1)S(1)} all-gather(bf16[1,2,5120]{2,1,0:T(2,128)(2,1)S(1)} %get-tuple-element.4), channel_id=1, replica_groups=mesh['group'=16,'tensor'=64] {'group'}, dimensions={0}, use_global_device_ids=true | all-gather | bytes 348160 | tf_op jit(solution)/shard_map/all_gather | solution.py:55
  405.6 0.1 reshape.32
  405.7 10.9 %fusion.3 = bf16[1,32,1536]{2,1,0:T(8,128)(2,1)} fusion(bf16[32,5120]{1,0:T(8,128)(2,1)S(1)} %reshape.32, bf16[1536,5120]{1,0:T(8,128)(2,1)} %all-gather.3.cloned.1.call-done, bf16[1,32,1536]{2,1,0:T(8,128)(2,1)S(1)} %copy-done.1, pred[1536]{0:T(1024)(128)(4,1)S(1)} %gt.21), kind=kOutput, calls=%fused_computation.5 | convolution fusion | flops 503414784 | bytes 16254464 | tf_op jit(solution)/shard_map/dot_general | solution.py:39
  (5 shorter events, 0.0 us)
Async XLA Ops:
  7.2 210.0 %copy-start = (bf16[32,1536]{1,0:T(8,128)(2,1)S(1)}, bf16[32,1536]{1,0:T(8,128)(2,1)}, u32[]{:S(2)}) copy-start(bf16[32,1536]{1,0:T(8,128)(2,1)} %param.10) | copy-start | bytes 294916
  7.2 219.0 %copy-start.5 = (s32[1,96]{1,0:T(1,128)S(1)}, s32[1,96]{1,0:T(1,128)}, u32[]{:S(2)}) copy-start(s32[1,96]{1,0:T(1,128)} %param.15) | copy-start | bytes 1156
  7.2 364.0 %copy-start.2 = (f32[2,5120]{1,0:T(2,128)S(1)}, f32[2,5120]{1,0:T(2,128)}, u32[]{:S(2)}) copy-start(f32[2,5120]{1,0:T(2,128)} %param.11) | copy-start | bytes 122884
  7.2 364.0 %copy-start.3 = (f32[2,5120]{1,0:T(2,128)S(1)}, f32[2,5120]{1,0:T(2,128)}, u32[]{:S(2)}) copy-start(f32[2,5120]{1,0:T(2,128)} %param.13) | copy-start | bytes 122884
  7.2 364.0 %copy-start.4 = (f32[2,5120]{1,0:T(2,128)S(1)}, f32[2,5120]{1,0:T(2,128)}, u32[]{:S(2)}) copy-start(f32[2,5120]{1,0:T(2,128)} %param.12) | copy-start | bytes 122884
  7.2 398.5 %copy-start.1 = (bf16[1,32,1536]{2,1,0:T(8,128)(2,1)S(1)}, bf16[1,32,1536]{2,1,0:T(8,128)(2,1)}, u32[]{:S(2)}) copy-start(bf16[1,32,1536]{2,1,0:T(8,128)(2,1)} %param.14) | copy-start | bytes 294916
  7.2 209.9 %all-gather.3.cloned.1.call-start = ((), (), s32[]{:S(2)}) async-start(), calls=%async_computation | async-start | bytes 15974400 | tf_op jit(solution)/shard_map/all_gather | solution.py:50
  10.2 360.9 %all-reduce.2.cloned.1.call-start = ((), (), s32[]{:S(2)}) async-start(), calls=%async_computation.1 | async-start | bytes 655360 | tf_op jit(solution)/shard_map/psum | solution.py:20
Sparse Core Ops, SparseCore 0:
  12.5 204.6 all-gather.2
  226.3 144.7 all-reduce.1
where the time goes:
time: 424 us; the launch traced here: 423 us
  waiting for transfers between devices  352 us (83%)
  blocking collectives  32.7 us (8%)
  matrix products  19.9 us (5%)
  between operations  14.1 us (3%)
  other arithmetic  4.61 us (1%)
    all_gather x1, waiting for transfers between devices, local(): normed_all = lax.all_gather(normed_local, 'tensor', axis=0, tiled=True)  207 us
    psum x1, waiting for transfers between devices, broadcast(): return lax.psum(kept, axis)  145 us
    all_gather x1, blocking collectives, local(): lax.all_gather(new_master.astype(jnp.bfloat16), 'group', axis=0, tiled=True)  32.7 us
    dot_general x1, matrix products, project(): lax.dot_general(weights, normed_rows, (((1,), (1,)), ((), ())), preferred...  10.9 us
    dot_general x1, matrix products, local(): jnp.dot(cotangent, normed_all, preferred_element_type=jnp.float32)  9.02 us
  transfers between devices with their start and end apart: 2, of which 2 were waited for; matrix products, arithmetic and copies ran while one was open for 0% of the time, Pallas kernels for 0%

commit v1 on v0

v1 whole, which is shorter than its diff:
```python
import jax
import jax.numpy as jnp
from jax import lax
from jax.experimental import pallas as pl
from jax.experimental.pallas import tpu as pltpu
from jax.sharding import PartitionSpec as P

PAGE = 16
D = 5120
ROWS = 1536
NZ = 16
NG = 16
DEV_ROWS = 24
CHIP_ROWS = 48
HALF = D // 2
QUARTER = D // 4
SLICE = D // 8
PLANE_CH = 128

learning_rate = 0.003
first_decay = 0.9
second_decay = 0.999
adam_epsilon = 1e-08
norm_epsilon = 1e-06
second_correction = 0.632304575229

MESH = pl.DeviceIdType.MESH
F32 = jnp.float32
BF16 = jnp.bfloat16


def select_matrix(shape, source_of_row):
    row = lax.broadcasted_iota(jnp.int32, shape, 0)
    col = lax.broadcasted_iota(jnp.int32, shape, 1)
    return jnp.where(col == source_of_row(row), 1.0, 0.0).astype(BF16)


def kernel(
    hidden, gain, cot, master, first, second, old, stale,
    new_master, new_first, new_second, cache,
    nsend, ncore, nmine, nbuf, n0, cots, cotp, gsend, grecv, g2send, g2, wsend, w1, wtile, wbuf,
    obuf, o1, osum, o2send, o2,
    core_s, core_r, x_s, x_r, ring_s, ring_r, cot_s, cot_r, l1_s, l1_r, l2_s, l2_r, l3_s, l3_r,
    l5_s, l5_r, l6_s, l6_r, w1_s, w1_r, w2_s, w2_r, o1_s, o1_r, o2_s, o2_r,
):
    g = lax.axis_index("group")
    t = lax.axis_index("tensor")
    xl = g // 8
    y = g % 8
    z = t // 4
    p = t % 4
    xh = p // 2
    co = p % 2

    def dev(group, tensor):
        return (group, tensor)

    def at_z(offset):
        return dev(g, ((z + offset + NZ) % NZ) * 4 + p)

    def at_plane(other):
        return dev(g, z * 4 + other)

    sibling = at_plane(2 * xh + (1 - co))
    partner = at_plane(2 * (1 - xh) + co)

    def copy(src, dst, ss, rs, where):
        return pltpu.make_async_remote_copy(
            src_ref=src, dst_ref=dst, send_sem=ss, recv_sem=rs, device_id=where, device_id_type=MESH
        )

    barrier = pltpu.get_barrier_semaphore()
    greet = [at_z(o) for o in (1, -1, 2, -2, 4, -4, 8)]
    greet += [at_plane((p + k) % 4) for k in (1, 2, 3)]
    greet += [dev((g + k) % NG, t) for k in range(1, NG)]
    for where in greet:
        pl.semaphore_signal(barrier, inc=1, device_id=where, device_id_type=MESH)

    values = hidden[0].astype(F32)
    inverse = lax.rsqrt(jnp.mean(values * values, axis=-1, keepdims=True) + norm_epsilon)
    normed = (values * inverse * gain[...]).astype(BF16)
    for h in range(2):
        nsend[h, 0:DEV_ROWS] = normed[:, h * HALF:(h + 1) * HALF]
        nsend[h, DEV_ROWS:32] = jnp.zeros((8, HALF), BF16)
    ncore[co] = nsend[co]

    pl.semaphore_wait(barrier, len(greet))

    core_out = copy(nsend.at[1 - co], ncore.at[co], core_s, core_r, sibling)
    core_out.start()
    lane = 2 * xl + y // 4
    cot_out = copy(cot, cots.at[p], cot_s, cot_r.at[p], at_plane(lane))

    @pl.when(p != lane)
    def _():
        cot_out.start()

    core_in = copy(nsend.at[1 - co], ncore.at[1 - co], core_s, core_r, sibling)
    core_in.wait_recv()
    for s in range(2):
        for c in range(2):
            nmine[s, c * DEV_ROWS:(c + 1) * DEV_ROWS] = ncore[c, 0:DEV_ROWS, s * QUARTER:(s + 1) * QUARTER]

    def ring(direction, step, chunk):
        sign = 1 if direction == 0 else -1
        slot = (z - sign * step + NZ) % NZ
        row = xh if chunk == 0 else 1 - xh
        src = nbuf.at[slot, row]
        if step == 0 and chunk == 0:
            src = nmine.at[xh]
        return copy(
            src, nbuf.at[slot, row], ring_s.at[direction, step, chunk], ring_r.at[direction, step, chunk],
            at_z(sign),
        )

    def ring_in(direction, step, chunk):
        sign = 1 if direction == 0 else -1
        slot = (z - sign * (step + 1) + NZ) % NZ
        row = xh if chunk == 0 else 1 - xh
        return copy(
            nbuf.at[slot, row], nbuf.at[slot, row], ring_s.at[direction, step, chunk],
            ring_r.at[direction, step, chunk], at_z(-sign),
        )

    def steps(direction, chunk):
        return 8 if direction == chunk else 7

    for d in range(2):
        ring(d, 0, 0).start()
    x_out = copy(nmine.at[1 - xh], nbuf.at[z, xh], x_s, x_r, partner)
    x_out.start()

    def l1(j):
        target = 8 * xh + 4 * co + j
        return copy(
            nmine.at[j // 2, :, (j % 2) * SLICE:(j % 2 + 1) * SLICE], n0.at[z, xh],
            l1_s.at[j], l1_r, dev(target, t),
        )

    for j in range(4):
        @pl.when((g == 0) & ((p != 0) | (j != 0)))
        def _():
            l1(j).start()

    @pl.when((g == 0) & (p == 0))
    def _():
        n0[z, 0] = nmine[0, :, 0:SLICE]

    nbuf[z, xh] = nmine[xh]
    is_lane = p == lane

    @pl.when(is_lane)
    def _():
        for k in range(NZ):
            n0[k, 1 - xl] = jnp.zeros((CHIP_ROWS, SLICE), BF16)
        cots[p] = cot[...]
        for k in range(1, 4):
            other = (p + k) % 4
            copy(cot, cots.at[other], cot_s, cot_r.at[other], at_plane(other)).wait_recv()
        order = select_matrix((PLANE_CH, PLANE_CH), lambda i: ((i // 2) % 4) * 32 + (i // 8) * 2 + i % 2)
        cotp[...] = jnp.dot(
            order, cots[...].reshape(PLANE_CH, ROWS), preferred_element_type=F32
        ).astype(BF16)

    copy(nmine.at[xh], nbuf.at[z, 1 - xh], x_s, x_r, partner).wait_recv()
    for d in range(2):
        ring(d, 0, 1).start()

    def ring_step(step):
        for chunk in range(2):
            for d in range(2):
                if step - 1 < steps(d, chunk):
                    ring_in(d, step - 1, chunk).wait_recv()
                if step < steps(d, chunk):
                    ring(d, step, chunk).start()

    def l2(k):
        return copy(n0.at[z, xl], n0.at[z, xl], l2_s.at[k], l2_r.at[k], at_z(4 * (k + 1)))

    def l2_in(k):
        slot = (z - 4 * (k + 1) + NZ) % NZ
        return copy(n0.at[slot, xl], n0.at[slot, xl], l2_s.at[k], l2_r.at[k], at_z(-4 * (k + 1)))

    n0q = n0.reshape(4, 4, 2, CHIP_ROWS, SLICE)
    hops = ((1, 0, 4), (-1, 0, 4), (2, 0, 2), (-2, 2, 2))

    def l3(k, arriving):
        offset, start, size = hops[k]
        b = (z - offset + NZ) % 4 if arriving else z % 4
        ref = n0q.at[start:start + size, b, xl]
        return copy(ref, ref, l3_s.at[k], l3_r.at[k], at_z(-offset if arriving else offset))

    @pl.when(is_lane)
    def _():
        @pl.when((g != 0) | (p != 0))
        def _():
            copy(n0.at[z, xl], n0.at[z, xl], l1_s.at[0], l1_r, dev((g + 1) % NG, t)).wait_recv()
        for k in range(3):
            l2(k).start()

    ring_step(1)

    @pl.when(is_lane)
    def _():
        for k in range(3):
            l2_in(k).wait_recv()
        for k in range(4):
            l3(k, False).start()

    ring_step(2)

    def l5(k):
        return copy(
            gsend.at[k], grecv.at[y % 4], l5_s.at[k], l5_r.at[y % 4], dev(k, t)
        )

    @pl.when(is_lane)
    def _():
        for k in range(4):
            l3(k, True).wait_recv()
        gsend[...] = jnp.dot(
            cotp[...], n0[...].reshape(ROWS, SLICE), preferred_element_type=F32
        ).reshape(NG, 8, SLICE)
        for k in range(NG):
            @pl.when(g != k)
            def _():
                l5(k).start()
        grecv[y % 4] = gsend[g]

    ring_step(3)

    for j in range(4):
        origin = 8 * xh + 4 * co + j

        @pl.when(g != origin)
        def _():
            copy(gsend.at[0], grecv.at[j], l5_s.at[0], l5_r.at[j], dev(origin, t)).wait_recv()

    for k in range(4):
        for j in range(4):
            g2send[k, j] = grecv[j, 2 * k:2 * k + 2]
    for k in range(1, 4):
        other = (p + k) % 4
        copy(g2send.at[other], g2.at[p], l6_s.at[k - 1], l6_r.at[p], at_plane(other)).start()
    g2[p] = g2send[p]
    for k in range(1, 4):
        other = (p + k) % 4
        copy(g2send.at[p], g2.at[other], l6_s.at[k - 1], l6_r.at[other], at_plane(other)).wait_recv()

    for c in range(2):
        for j in range(4):
            cols = slice((4 * c + j) * SLICE, (4 * c + j + 1) * SLICE)
            gradient = g2[c, j] + g2[2 + c, j]
            m = first_decay * first[:, cols] + (1.0 - first_decay) * gradient
            v = second_decay * second[:, cols] + (1.0 - second_decay) * gradient * gradient
            w = master[:, cols] - learning_rate * (m / (jnp.sqrt(v / second_correction) + adam_epsilon))
            new_first[:, cols] = m
            new_second[:, cols] = v
            new_master[:, cols] = w
            wsend[2 * c + j // 2, :, (j % 2) * SLICE:(j % 2 + 1) * SLICE] = w

    def quarter_of(q):
        return 2 * (q % 2) + q // 2

    for k in range(1, 4):
        other = (p + k) % 4
        copy(wsend.at[quarter_of(other)], w1.at[p], w1_s.at[k - 1], w1_r.at[p], at_plane(other)).start()
    w1[p] = wsend[quarter_of(p)]

    ring_step(4)

    for k in range(1, 4):
        other = (p + k) % 4
        copy(w1.at[other], w1.at[other], w1_s.at[k - 1], w1_r.at[other], at_plane(other)).wait_recv()
    wtile[...] = jnp.concatenate([w1[k] for k in range(4)], axis=0).astype(BF16)
    for k in range(1, NG):
        copy(wtile, wbuf.at[g], w2_s.at[k - 1], w2_r.at[g], dev((g + k) % NG, t)).start()
    wbuf[g] = wtile[...]

    ring_step(5)
    ring_step(6)
    ring_step(7)

    for k in range(1, NG):
        other = (g + k) % NG
        copy(wtile, wbuf.at[other], w2_s.at[k - 1], w2_r.at[other], dev(other, t)).wait_recv()
    back = select_matrix((PLANE_CH, PLANE_CH), lambda c: ((c % 32) // 2) * 8 + (c // 32) * 2 + c % 2)
    weights = jnp.dot(
        back, wbuf[...].astype(F32).reshape(PLANE_CH, QUARTER).astype(BF16), preferred_element_type=F32
    ).astype(BF16)

    ring_step(8)

    for k in range(6):
        rows = slice(256 * k, 256 * (k + 1))
        block = nbuf[...].reshape(ROWS, QUARTER)[rows]
        obuf[:, :, :, rows] = lax.dot_general(
            weights, block, (((1,), (1,)), ((), ())), preferred_element_type=F32
        ).reshape(2, 2, 32, 256)

    o1_out = copy(obuf.at[:, 1 - co], o1, o1_s, o1_r, sibling)
    o1_out.start()
    expand = jnp.where(
        lax.broadcasted_iota(jnp.int32, (ROWS // PAGE, ROWS), 1) // PAGE
        == lax.broadcasted_iota(jnp.int32, (ROWS // PAGE, ROWS), 0),
        1.0, 0.0,
    ).astype(BF16)
    marks = jnp.broadcast_to(stale[...].astype(F32), (8, ROWS // PAGE)).astype(BF16)
    mask = jnp.dot(marks, expand, preferred_element_type=F32)[0:1]
    o1_out.wait_recv()
    for k in range(2):
        osum[k] = obuf[k, co] + o1[k]
    o2send[...] = osum[1 - xh].astype(BF16)
    o2_out = copy(o2send, o2, o2_s, o2_r, partner)
    o2_out.start()
    o2_out.wait_recv()
    result = (osum[xh] + o2[...].astype(F32)).astype(BF16)
    cache[0] = jnp.where(mask > 0.5, result, old[0])

    core_out.wait_send()
    x_out.wait_send()

    @pl.when(p != lane)
    def _():
        cot_out.wait_send()

    for step in range(8):
        for chunk in range(2):
            for d in range(2):
                if step < steps(d, chunk):
                    ring(d, step, chunk).wait_send()
    for j in range(4):
        @pl.when((g == 0) & ((p != 0) | (j != 0)))
        def _():
            l1(j).wait_send()

    @pl.when(is_lane)
    def _():
        for k in range(3):
            l2(k).wait_send()
        for k in range(4):
            l3(k, False).wait_send()
        for k in range(NG):
            @pl.when(g != k)
            def _():
                l5(k).wait_send()

    for k in range(1, 4):
        other = (p + k) % 4
        copy(g2send.at[other], g2.at[p], l6_s.at[k - 1], l6_r.at[p], at_plane(other)).wait_send()
        copy(wsend.at[quarter_of(other)], w1.at[p], w1_s.at[k - 1], w1_r.at[p], at_plane(other)).wait_send()
    for k in range(1, NG):
        copy(wtile, wbuf.at[g], w2_s.at[k - 1], w2_r.at[g], dev((g + k) % NG, t)).wait_send()
    o1_out.wait_send()
    o2_out.wait_send()


def local(hidden, norm_gain, cotangent, master, first_moment, second_moment, old_cache, stale_pages):
    dma = pltpu.SemaphoreType.DMA
    vmem = pl.BlockSpec(memory_space=pltpu.VMEM)
    state = jax.ShapeDtypeStruct((2, D), F32)
    scratch = [
        pltpu.VMEM((2, 32, HALF), BF16),
        pltpu.VMEM((2, 32, HALF), BF16),
        pltpu.VMEM((2, CHIP_ROWS, QUARTER), BF16),
        pltpu.VMEM((NZ, 2, CHIP_ROWS, QUARTER), BF16),
        pltpu.VMEM((NZ, 2, CHIP_ROWS, SLICE), BF16),
        pltpu.VMEM((4, 32, ROWS), BF16),
        pltpu.VMEM((PLANE_CH, ROWS), BF16),
        pltpu.VMEM((NG, 8, SLICE), F32),
        pltpu.VMEM((4, 8, SLICE), F32),
        pltpu.VMEM((4, 4, 2, SLICE), F32),
        pltpu.VMEM((4, 4, 2, SLICE), F32),
        pltpu.VMEM((4, 2, QUARTER), F32),
        pltpu.VMEM((4, 2, QUARTER), F32),
        pltpu.VMEM((8, QUARTER), BF16),
        pltpu.VMEM((NG, 8, QUARTER), BF16),
        pltpu.VMEM((2, 2, 32, ROWS), F32),
        pltpu.VMEM((2, 32, ROWS), F32),
        pltpu.VMEM((2, 32, ROWS), F32),
        pltpu.VMEM((32, ROWS), BF16),
        pltpu.VMEM((32, ROWS), BF16),
        dma, dma, dma, dma, dma((2, 8, 2)), dma((2, 8, 2)), dma, dma((4,)), dma((4,)), dma,
        dma((3,)), dma((3,)), dma((4,)), dma((4,)),
        dma((NG,)), dma((4,)), dma((3,)), dma((4,)), dma((3,)), dma((4,)), dma((NG - 1,)), dma((NG,)),
        dma, dma, dma, dma,
    ]
    return pl.pallas_call(
        kernel,
        out_shape=(state, state, state, jax.ShapeDtypeStruct(old_cache.shape, BF16)),
        in_specs=[vmem] * 8,
        out_specs=(vmem,) * 4,
        scratch_shapes=scratch,
        compiler_params=pltpu.CompilerParams(
            collective_id=0, has_side_effects=True, vmem_limit_bytes=48 * 1024 * 1024
        ),
        cost_estimate=pl.CostEstimate(flops=800_000_000, bytes_accessed=2_000_000, transcendentals=20_000),
    )(
        hidden, norm_gain.reshape(1, D), cotangent, master, first_moment, second_moment, old_cache, stale_pages
    )


def solution(mesh):
    placed = (
        P("group", "tensor", None),
        P(),
        P("tensor", None),
        P(("tensor", "group"), None),
        P(("tensor", "group"), None),
        P(("tensor", "group"), None),
        P("group", "tensor", None),
        P("group", None),
    )
    return jax.shard_map(
        local,
        mesh=mesh,
        in_specs=placed,
        out_specs=(
            P(("tensor", "group"), None),
            P(("tensor", "group"), None),
            P(("tensor", "group"), None),
            P("group", "tensor", None),
        ),
        check_vma=False,
    )
```

time: 424 us -> 106 us (0.25)
  the two profiles are of different devices: /device:TPU:6 before, /device:TPU:1 now
where the time goes in v1:
time: 106 us; the launch traced here: 105 us
  Pallas kernels  95.7 us (90%)
  local copies, waits for them, and re-layouts  8.93 us (8%)
    pallas_call x1, Pallas kernels, local(): pl.pallas_call(kernel, out_shape=(state, state, state, jax.ShapeDtypeStru...  95.7 us
    unnamed x20, local copies, waits for them, and re-layouts  8.93 us

profile of v1, /device:TPU:1, one launch (start us, length us, event | category | flops | bytes accessed | tf_op | source)
XLA Modules:
  0.0 105.3 jit_solution(3309843442443230368)
XLA Ops:
  0.6 0.0 copy-start.7
  0.6 0.6 copy-done.7
  1.3 0.0 copy-start
  1.3 0.9 copy-done
  2.2 0.0 copy-start.1
  2.2 0.9 copy-done.1
  3.1 0.0 copy-start.2
  3.1 0.9 copy-done.2
  4.0 0.0 copy-start.3
  4.0 0.8 copy-done.3
  4.8 0.0 copy-start.4
  4.8 0.8 copy-done.4
  5.6 0.0 copy-start.5
  5.6 0.8 copy-done.5
  6.4 0.0 copy-start.6
  6.4 0.7 copy-done.6
  7.1 95.7 %shard_map.111 = (f32[2,5120]{1,0:T(2,128)S(1)}, f32[2,5120]{1,0:T(2,128)S(1)}, f32[2,5120]{1,0:T(2,128)S(1)}, bf16[1,32,1536]{2,1,0:T(8,128)(2,1)S(1)}) custom-call(bf16[1,24,5120]{2,1,0:T(8,128)(2,1)S(1)} %copy-done, f32[1,5120]{1,0:T(1,128)S(1)} %bitcast.1, bf16[32,1536]{1,0:T(8,128)(2,1)S(1)} %copy-done.1, f32[2,5120]{1,0:T(2,128)S(1)} %copy-done.3, ...), custom_call_target="tpu_custom_call" | custom-call | flops 800000000 | bytes 2000000 | tf_op jit(solution)/shard_map/pallas_call | solution.py:388
  102.8 0.6 copy.16
  103.4 0.6 copy.17
  104.0 0.6 copy.18
  104.6 0.6 copy.19
Async XLA Ops:
  0.6 0.7 copy-start.7
  1.3 0.9 copy-start
  2.2 0.9 copy-start.1
  3.1 0.9 copy-start.2
  4.0 0.8 copy-start.3
  4.8 0.8 copy-start.4
  5.6 0.8 copy-start.5
  6.4 0.7 copy-start.6

commit v2 on v1

v2 whole, which is shorter than its diff:
```python
import jax
import jax.numpy as jnp
from jax import lax
from jax.experimental import pallas as pl
from jax.experimental.pallas import tpu as pltpu
from jax.sharding import PartitionSpec as P

PAGE = 16
D = 5120
ROWS = 1536
NZ = 16
NG = 16
DEV_ROWS = 24
CHIP_ROWS = 48
HALF = D // 2
QUARTER = D // 4
SLICE = D // 8
WIDTHS = (384, 256)
PLANE_CH = 128

learning_rate = 0.003
first_decay = 0.9
second_decay = 0.999
adam_epsilon = 1e-08
norm_epsilon = 1e-06
second_correction = 0.632304575229

MESH = pl.DeviceIdType.MESH
F32 = jnp.float32
BF16 = jnp.bfloat16


def select_matrix(shape, source_of_row):
    row = lax.broadcasted_iota(jnp.int32, shape, 0)
    col = lax.broadcasted_iota(jnp.int32, shape, 1)
    return jnp.where(col == source_of_row(row), 1.0, 0.0).astype(BF16)


def kernel(
    hidden, gain, cot, master, first, second, old, stale,
    new_master, new_first, new_second, cache,
    hidden_v, gain_v, old_v, stale_v, nsend, ncore, nmine, nbuf, n0, cots, cotp, gsend, grecv, state, newstate,
    wtile, wbuf, obuf, o1, osum, o2send, o2,
    in_s, core_s, core_r, x_s, x_r, ring_s, ring_r, cot_s, cot_r, st_s, st_r, l1_s, l1_r, l2_s, l2_r, l3_s, l3_r,
    l5_s, l5_r, back_s, back_r, w2_s, w2_r, o1_s, o1_r, o2_s, o2_r,
):
    g = lax.axis_index("group")
    t = lax.axis_index("tensor")
    xl = g // 8
    y = g % 8
    z = t // 4
    p = t % 4
    xh = p // 2
    co = p % 2

    def dev(group, tensor):
        return (group, tensor)

    def at_z(offset):
        return dev(g, ((z + offset + NZ) % NZ) * 4 + p)

    def at_plane(other):
        return dev(g, z * 4 + other)

    sibling = at_plane(2 * xh + (1 - co))
    across = 2 * (1 - xh) + co
    partner = at_plane(across)

    def copy(src, dst, ss, rs, where):
        return pltpu.make_async_remote_copy(
            src_ref=src, dst_ref=dst, send_sem=ss, recv_sem=rs, device_id=where, device_id_type=MESH
        )

    barrier = pltpu.get_barrier_semaphore()
    greet = [at_z(o) for o in (1, -1, 2, -2, 4, -4, 8)]
    greet += [at_plane((p + k) % 4) for k in (1, 2, 3)]
    greet += [dev((g + k) % NG, t) for k in range(1, NG)]
    greet += [dev((g + k) % NG, z * 4 + across) for k in range(1, NG)]
    for where in greet:
        pl.semaphore_signal(barrier, inc=1, device_id=where, device_id_type=MESH)

    def quarter_cols(q):
        return pl.ds(pl.multiple_of((2 * (q % 2) + q // 2) * QUARTER, QUARTER), QUARTER)

    lane_of = [2 * w + y // 4 for w in range(2)]
    is_lane = [p == lane_of[w] for w in range(2)]
    any_lane = co == y // 4

    load_hidden = pltpu.make_async_copy(hidden, hidden_v, in_s.at[0])
    load_gain = pltpu.make_async_copy(gain, gain_v, in_s.at[1])
    load_old = pltpu.make_async_copy(old, old_v, in_s.at[2])
    load_stale = pltpu.make_async_copy(stale, stale_v, in_s.at[3])
    load_cot = pltpu.make_async_copy(cot, cots.at[p], cot_r.at[p])
    load_hidden.start()
    load_gain.start()
    load_old.start()
    load_stale.start()
    pl.when(any_lane)(load_cot.start)
    states = (master, first, second)
    load_state = [pltpu.make_async_copy(states[k].at[:, quarter_cols(p)], state.at[k, p], st_r.at[k, p]) for k in range(3)]
    for load in load_state:
        load.start()

    load_hidden.wait()
    load_gain.wait()
    values = hidden_v[0].astype(F32)
    inverse = lax.rsqrt(jnp.mean(values * values, axis=-1, keepdims=True) + norm_epsilon)
    normed = (values * inverse * gain_v[...]).astype(BF16)
    for h in range(2):
        nsend[h, 0:DEV_ROWS] = normed[:, h * HALF:(h + 1) * HALF]
        nsend[h, DEV_ROWS:32] = jnp.zeros((8, HALF), BF16)
    ncore[co] = nsend[co]

    pl.semaphore_wait(barrier, len(greet))

    core_out = copy(nsend.at[1 - co], ncore.at[co], core_s, core_r, sibling)
    core_out.start()

    core_in = copy(nsend.at[1 - co], ncore.at[1 - co], core_s, core_r, sibling)
    core_in.wait_recv()
    for s in range(2):
        for c in range(2):
            nmine[s, c * DEV_ROWS:(c + 1) * DEV_ROWS] = ncore[c, 0:DEV_ROWS, s * QUARTER:(s + 1) * QUARTER]

    def ring(direction, step, chunk):
        sign = 1 if direction == 0 else -1
        slot = (z - sign * step + NZ) % NZ
        row = xh if chunk == 0 else 1 - xh
        src = nbuf.at[slot, row]
        if step == 0 and chunk == 0:
            src = nmine.at[xh]
        return copy(
            src, nbuf.at[slot, row], ring_s.at[direction, step, chunk], ring_r.at[direction, step, chunk],
            at_z(sign),
        )

    def ring_in(direction, step, chunk):
        sign = 1 if direction == 0 else -1
        slot = (z - sign * (step + 1) + NZ) % NZ
        row = xh if chunk == 0 else 1 - xh
        return copy(
            nbuf.at[slot, row], nbuf.at[slot, row], ring_s.at[direction, step, chunk],
            ring_r.at[direction, step, chunk], at_z(-sign),
        )

    def steps(direction, chunk):
        return 8 if direction == chunk else 7

    def l1(j, w):
        target = 8 * xh + 4 * co + j
        start = (j % 2) * SLICE + w * WIDTHS[0]
        return copy(
            nmine.at[j // 2, :, start:start + WIDTHS[w]], n0.at[z, xh, :, 0:WIDTHS[w]],
            l1_s.at[j, w], l1_r, dev(target, z * 4 + 2 * w + co),
        )

    def l1_cond(j, w):
        return (g == 0) & (p != 0) if (j, w) == (0, 0) else g == 0

    for j in range(4):
        for w in range(2):
            pl.when(l1_cond(j, w))(l1(j, w).start)
    x_out = copy(nmine.at[1 - xh], nbuf.at[z, xh], x_s, x_r, partner)
    x_out.start()
    for d in range(2):
        ring(d, 0, 0).start()

    def st(k, i):
        other = (p + i) % 4
        return copy(states[k].at[:, quarter_cols(other)], state.at[k, p], st_s.at[k, i - 1], st_r.at[k, p], at_plane(other))

    def cot_out(w):
        return copy(cot, cots.at[p], cot_s.at[w], cot_r.at[p], at_plane(lane_of[w]))

    for w in range(2):
        pl.when(p != lane_of[w])(cot_out(w).start)
    for i in range(1, 4):
        for k in range(3):
            st(k, i).start()

    @pl.when((g == 0) & (p == 0))
    def _():
        n0[z, 0] = nmine[0, :, 0:WIDTHS[0]]

    nbuf[z, xh] = nmine[xh]

    @pl.when(any_lane)
    def _():
        for k in range(NZ):
            n0[k, 1 - xl] = jnp.zeros((CHIP_ROWS, WIDTHS[0]), BF16)

    @pl.when(is_lane[1])
    def _():
        for k in range(NZ):
            n0[k, xl, :, WIDTHS[1]:WIDTHS[0]] = jnp.zeros((CHIP_ROWS, WIDTHS[0] - WIDTHS[1]), BF16)

    copy(nmine.at[xh], nbuf.at[z, 1 - xh], x_s, x_r, partner).wait_recv()
    for d in range(2):
        ring(d, 0, 1).start()

    def ring_step(step):
        for chunk in range(2):
            for d in range(2):
                if step - 1 < steps(d, chunk):
                    ring_in(d, step - 1, chunk).wait_recv()
                if step < steps(d, chunk):
                    ring(d, step, chunk).start()

    def l2(k, w):
        ref = n0.at[z, xl, :, 0:WIDTHS[w]]
        return copy(ref, ref, l2_s.at[k], l2_r.at[k], at_z(4 * (k + 1)))

    def l2_in(k, w):
        ref = n0.at[(z - 4 * (k + 1) + NZ) % NZ, xl, :, 0:WIDTHS[w]]
        return copy(ref, ref, l2_s.at[k], l2_r.at[k], at_z(-4 * (k + 1)))

    n0q = n0.reshape(4, 4, 2, CHIP_ROWS, WIDTHS[0])
    hops = ((1, 0, 4), (-1, 0, 4), (2, 0, 2), (-2, 2, 2))

    def l3(k, w, arriving):
        offset, start, size = hops[k]
        b = (z - offset + NZ) % 4 if arriving else z % 4
        ref = n0q.at[start:start + size, b, xl, :, 0:WIDTHS[w]]
        return copy(ref, ref, l3_s.at[k], l3_r.at[k], at_z(-offset if arriving else offset))

    for w in range(2):
        @pl.when(is_lane[w])
        def _(w=w):
            @pl.when((g != 0) | (p != 0))
            def _():
                ref = n0.at[z, xl, :, 0:WIDTHS[w]]
                copy(ref, ref, l1_s.at[0, 0], l1_r, dev((g + 1) % NG, t)).wait_recv()
            for k in range(3):
                l2(k, w).start()

    @pl.when(any_lane)
    def _():
        load_cot.wait()
        for k in range(1, 4):
            other = (p + k) % 4
            copy(cot, cots.at[other], cot_s.at[0], cot_r.at[other], at_plane(other)).wait_recv()
        order = select_matrix((PLANE_CH, PLANE_CH), lambda i: ((i // 2) % 4) * 32 + (i // 8) * 2 + i % 2)
        cotp[...] = jnp.dot(
            order, cots[...].reshape(PLANE_CH, ROWS), preferred_element_type=F32
        ).astype(BF16)

    ring_step(1)

    for w in range(2):
        @pl.when(is_lane[w])
        def _(w=w):
            for k in range(3):
                l2_in(k, w).wait_recv()
            for k in range(4):
                l3(k, w, False).start()

    ring_step(2)

    holder = 2 * ((y // 2) % 2) + y // 4

    def l5(k, w):
        return copy(
            gsend.at[k, :, 0:WIDTHS[w]], grecv.at[xl, y % 2, w, :, 0:WIDTHS[w]],
            l5_s.at[k], l5_r.at[xl, y % 2, w], dev(k, z * 4 + holder),
        )

    for w in range(2):
        @pl.when(is_lane[w])
        def _(w=w):
            for k in range(4):
                l3(k, w, True).wait_recv()

    @pl.when(any_lane)
    def _():
        gsend[...] = jnp.dot(
            cotp[...], n0[...].reshape(ROWS, WIDTHS[0]), preferred_element_type=F32
        ).reshape(NG, 8, WIDTHS[0]).astype(BF16)

    for w in range(2):
        @pl.when(is_lane[w])
        def _(w=w):
            for k in range(NG):
                pl.when((g != k) | (p != holder))(l5(k, w).start)

            @pl.when(p == holder)
            def _():
                grecv[xl, y % 2, w] = gsend[g]

    ring_step(3)

    for a in range(2):
        for j in range(2):
            for w in range(2):
                origin = 8 * a + 4 * co + 2 * xh + j
                lane = 2 * w + co

                @pl.when((g != origin) | (p != lane))
                def _(a=a, j=j, w=w, origin=origin, lane=lane):
                    ref = grecv.at[a, j, w, :, 0:WIDTHS[w]]
                    copy(ref, ref, l5_s.at[0], l5_r.at[a, j, w], dev(origin, z * 4 + lane)).wait_recv()
    for k in range(3):
        load_state[k].wait()
        for i in range(1, 4):
            other = (p + i) % 4
            copy(state.at[k, other], state.at[k, other], st_s.at[k, i - 1], st_r.at[k, other], at_plane(other)).wait_recv()

    parts = [
        jnp.concatenate(
            [grecv[a, j, w, :, 0:WIDTHS[w]].astype(F32) for j in range(2) for w in range(2)], axis=1
        )
        for a in range(2)
    ]
    gradient = parts[0] + parts[1]
    old_master, old_first, old_second = [
        jnp.concatenate([state[k, q] for q in range(4)], axis=0) for k in range(3)
    ]
    m = first_decay * old_first + (1.0 - first_decay) * gradient
    v = second_decay * old_second + (1.0 - second_decay) * gradient * gradient
    w_new = old_master - learning_rate * (m / (jnp.sqrt(v / second_correction) + adam_epsilon))
    wtile[...] = w_new.astype(BF16)
    for k in range(1, NG):
        copy(wtile, wbuf.at[g], w2_s.at[k - 1], w2_r.at[g], dev((g + k) % NG, t)).start()
    wbuf[g] = wtile[...]
    for k, value in enumerate((w_new, m, v)):
        for q in range(4):
            newstate[k, q] = value[2 * q:2 * q + 2]
    results = (new_master, new_first, new_second)

    def back(k, i):
        other = (p + i) % 4
        return copy(
            newstate.at[k, other], results[k].at[:, quarter_cols(p)], back_s.at[k, i - 1], back_r.at[k, p], at_plane(other)
        )

    keep = [
        pltpu.make_async_copy(newstate.at[k, p], results[k].at[:, quarter_cols(p)], back_r.at[k, p]) for k in range(3)
    ]
    for k in range(3):
        for i in range(1, 4):
            back(k, i).start()
        keep[k].start()

    ring_step(4)
    ring_step(5)
    ring_step(6)
    ring_step(7)

    expand = jnp.where(
        lax.broadcasted_iota(jnp.int32, (ROWS // PAGE, ROWS), 1) // PAGE
        == lax.broadcasted_iota(jnp.int32, (ROWS // PAGE, ROWS), 0),
        1.0, 0.0,
    ).astype(BF16)
    load_stale.wait()
    load_old.wait()
    marks = jnp.broadcast_to(stale_v[...].astype(F32), (8, ROWS // PAGE)).astype(BF16)
    mask = jnp.dot(marks, expand, preferred_element_type=F32)[0:1]

    for k in range(1, NG):
        other = (g + k) % NG
        copy(wtile, wbuf.at[other], w2_s.at[k - 1], w2_r.at[other], dev(other, t)).wait_recv()
    reorder = select_matrix((PLANE_CH, PLANE_CH), lambda c: ((c % 32) // 2) * 8 + (c // 32) * 2 + c % 2)
    weights = jnp.dot(
        reorder, wbuf[...].astype(F32).reshape(PLANE_CH, QUARTER).astype(BF16), preferred_element_type=F32
    ).astype(BF16)

    ring_step(8)

    for k in range(6):
        rows = slice(256 * k, 256 * (k + 1))
        block = nbuf[...].reshape(ROWS, QUARTER)[rows]
        obuf[:, :, :, rows] = lax.dot_general(
            weights, block, (((1,), (1,)), ((), ())), preferred_element_type=F32
        ).reshape(2, 2, 32, 256)

    def o1_copy(k):
        return copy(obuf.at[k, 1 - co], o1.at[k], o1_s.at[k], o1_r.at[k], sibling)

    o1_copy(1 - xh).start()
    o1_copy(xh).start()
    o1_copy(1 - xh).wait_recv()
    o2send[...] = (obuf[1 - xh, co] + o1[1 - xh]).astype(BF16)
    o2_out = copy(o2send, o2, o2_s, o2_r, partner)
    o2_out.start()
    o1_copy(xh).wait_recv()
    osum[...] = obuf[xh, co] + o1[xh]
    o2_out.wait_recv()
    result = (osum[...] + o2[...].astype(F32)).astype(BF16)
    cache[0] = jnp.where(mask > 0.5, result, old_v[0])

    for k in range(3):
        keep[k].wait()
        for i in range(1, 4):
            other = (p + i) % 4
            copy(
                newstate.at[k, p], results[k].at[:, quarter_cols(other)], back_s.at[k, i - 1], back_r.at[k, other],
                at_plane(other),
            ).wait_recv()
            back(k, i).wait_send()
            st(k, i).wait_send()
    core_out.wait_send()
    x_out.wait_send()
    for w in range(2):
        pl.when(p != lane_of[w])(cot_out(w).wait_send)
    for step in range(8):
        for chunk in range(2):
            for d in range(2):
                if step < steps(d, chunk):
                    ring(d, step, chunk).wait_send()
    for j in range(4):
        for w in range(2):
            pl.when(l1_cond(j, w))(l1(j, w).wait_send)
    for w in range(2):
        @pl.when(is_lane[w])
        def _(w=w):
            for k in range(3):
                l2(k, w).wait_send()
            for k in range(4):
                l3(k, w, False).wait_send()
            for k in range(NG):
                pl.when((g != k) | (p != holder))(l5(k, w).wait_send)
    for k in range(1, NG):
        copy(wtile, wbuf.at[g], w2_s.at[k - 1], w2_r.at[g], dev((g + k) % NG, t)).wait_send()
    o1_copy(1 - xh).wait_send()
    o1_copy(xh).wait_send()
    o2_out.wait_send()


def local(hidden, norm_gain, cotangent, master, first_moment, second_moment, old_cache, stale_pages):
    dma = pltpu.SemaphoreType.DMA
    vmem = pl.BlockSpec(memory_space=pltpu.VMEM)
    hbm = pl.BlockSpec(memory_space=pl.ANY)
    state = jax.ShapeDtypeStruct((2, D), F32)
    scratch = [
        pltpu.VMEM((1, DEV_ROWS, D), BF16),
        pltpu.VMEM((1, D), F32),
        pltpu.VMEM((1, 32, ROWS), BF16),
        pltpu.VMEM((1, ROWS // PAGE), jnp.int32),
        pltpu.VMEM((2, 32, HALF), BF16),
        pltpu.VMEM((2, 32, HALF), BF16),
        pltpu.VMEM((2, CHIP_ROWS, QUARTER), BF16),
        pltpu.VMEM((NZ, 2, CHIP_ROWS, QUARTER), BF16),
        pltpu.VMEM((NZ, 2, CHIP_ROWS, WIDTHS[0]), BF16),
        pltpu.VMEM((4, 32, ROWS), BF16),
        pltpu.VMEM((PLANE_CH, ROWS), BF16),
        pltpu.VMEM((NG, 8, WIDTHS[0]), BF16),
        pltpu.VMEM((2, 2, 2, 8, WIDTHS[0]), BF16),
        pltpu.VMEM((3, 4, 2, QUARTER), F32),
        pltpu.VMEM((3, 4, 2, QUARTER), F32),
        pltpu.VMEM((8, QUARTER), BF16),
        pltpu.VMEM((NG, 8, QUARTER), BF16),
        pltpu.VMEM((2, 2, 32, ROWS), F32),
        pltpu.VMEM((2, 32, ROWS), F32),
        pltpu.VMEM((32, ROWS), F32),
        pltpu.VMEM((32, ROWS), BF16),
        pltpu.VMEM((32, ROWS), BF16),
        dma((4,)), dma, dma, dma, dma, dma((2, 8, 2)), dma((2, 8, 2)), dma((2,)), dma((4,)),
        dma((3, 3)), dma((3, 4)), dma((4, 2)), dma,
        dma((3,)), dma((3,)), dma((4,)), dma((4,)),
        dma((NG,)), dma((2, 2, 2)), dma((3, 3)), dma((3, 4)), dma((NG - 1,)), dma((NG,)),
        dma((2,)), dma((2,)), dma, dma,
    ]
    return pl.pallas_call(
        kernel,
        out_shape=(state, state, state, jax.ShapeDtypeStruct(old_cache.shape, BF16)),
        in_specs=[hbm] * 8,
        out_specs=(vmem,) * 4,
        scratch_shapes=scratch,
        compiler_params=pltpu.CompilerParams(
            collective_id=0, has_side_effects=True, vmem_limit_bytes=56 * 1024 * 1024
        ),
        cost_estimate=pl.CostEstimate(flops=800_000_000, bytes_accessed=2_000_000, transcendentals=20_000),
    )(
        hidden, norm_gain.reshape(1, D), cotangent, master, first_moment, second_moment, old_cache, stale_pages
    )


def solution(mesh):
    placed = (
        P("group", "tensor", None),
        P(),
        P("tensor", None),
        P(("tensor", "group"), None),
        P(("tensor", "group"), None),
        P(("tensor", "group"), None),
        P("group", "tensor", None),
        P("group", None),
    )
    return jax.shard_map(
        local,
        mesh=mesh,
        in_specs=placed,
        out_specs=(
            P(("tensor", "group"), None),
            P(("tensor", "group"), None),
            P(("tensor", "group"), None),
            P("group", "tensor", None),
        ),
        check_vma=False,
    )
```

time: 106 us -> 92.5 us (0.87)
  Pallas kernels: 95.7 us -> 88.3 us
  local copies, waits for them, and re-layouts: 8.93 us -> 3.3 us
    pallas_call x1, Pallas kernels: 95.7 us -> 88.3 us  [local(): pl.pallas_call(kernel, out_shape=(state, state, state, jax.ShapeDtypeStru...]
    unnamed x20 -> x10, local copies, waits for them, and re-layouts: 8.93 us -> 3.3 us
where the time goes in v2:
time: 92.5 us; the launch traced here: 92.3 us
  Pallas kernels  88.3 us (95%)
  local copies, waits for them, and re-layouts  3.3 us (4%)
    pallas_call x1, Pallas kernels, local(): pl.pallas_call(kernel, out_shape=(state, state, state, jax.ShapeDtypeStru...  88.3 us
    unnamed x10, local copies, waits for them, and re-layouts  3.3 us

profile of v2, /device:TPU:1, one launch (start us, length us, event | category | flops | bytes accessed | tf_op | source)
XLA Modules:
  0.0 92.3 jit_solution(11408389044084807439)
XLA Ops:
  0.6 88.3 %shard_map.111 = (f32[2,5120]{1,0:T(2,128)}, f32[2,5120]{1,0:T(2,128)}, f32[2,5120]{1,0:T(2,128)}, bf16[1,32,1536]{2,1,0:T(8,128)(2,1)}) custom-call(bf16[1,24,5120]{2,1,0:T(8,128)(2,1)} %hidden.1, f32[1,5120]{1,0:T(1,128)} %bitcast.1, bf16[32,1536]{1,0:T(8,128)(2,1)} %cot.1, f32[2,5120]{1,0:T(2,128)} %master.1, f32[2,5120]{1,0:T(2,128)} %first.1, ...), custom_call_target="tpu_custom_call" | custom-call | flops 800000000 | bytes 2000000 | tf_op jit(solution)/shard_map/pallas_call | solution.py:462
  88.9 0.0 copy-start.2
  88.9 0.0 copy-start.1
  89.0 1.4 %copy.16 = f32[2,5120]{1,0:T(2,128)} copy(f32[2,5120]{1,0:T(2,128)} %get-tuple-element.8) | data formatting | bytes 81920
  90.4 0.0 copy-done.2
  90.4 0.0 copy-start
  90.4 0.6 copy.17
  91.0 0.0 copy-done.1
  91.0 0.6 copy.18
  91.6 0.0 copy-done
  91.6 0.6 copy.19
Async XLA Ops:
  88.9 1.4 %copy-start.2 = (f32[2,5120]{1,0:T(2,128)S(1)}, f32[2,5120]{1,0:T(2,128)}, u32[]{:S(2)}) copy-start(f32[2,5120]{1,0:T(2,128)} %get-tuple-element.9) | copy-start | bytes 122884
  88.9 2.1 %copy-start.1 = (f32[2,5120]{1,0:T(2,128)S(1)}, f32[2,5120]{1,0:T(2,128)}, u32[]{:S(2)}) copy-start(f32[2,5120]{1,0:T(2,128)} %get-tuple-element.10) | copy-start | bytes 122884
  90.4 1.2 %copy-start = (bf16[1,32,1536]{2,1,0:T(8,128)(2,1)S(1)}, bf16[1,32,1536]{2,1,0:T(8,128)(2,1)}, u32[]{:S(2)}) copy-start(bf16[1,32,1536]{2,1,0:T(8,128)(2,1)} %get-tuple-element.11) | copy-start | bytes 294916

commit v3 on v2

--- a/solution.py
+++ b/solution.py
@@ -38,11 +38,11 @@
 
 def kernel(
     hidden, gain, cot, master, first, second, old, stale,
-    new_master, new_first, new_second, cache,
+    new_state, cache,
     hidden_v, gain_v, old_v, stale_v, nsend, ncore, nmine, nbuf, n0, cots, cotp, gsend, grecv, state, newstate,
-    wtile, wbuf, obuf, o1, osum, o2send, o2,
+    wtile, wbuf, wmat, oall, opart, orecv, joined,
     in_s, core_s, core_r, x_s, x_r, ring_s, ring_r, cot_s, cot_r, st_s, st_r, l1_s, l1_r, l2_s, l2_r, l3_s, l3_r,
-    l5_s, l5_r, back_s, back_r, w2_s, w2_r, o1_s, o1_r, o2_s, o2_r,
+    l5_s, l5_r, back_s, back_r, w2_s, w2_r, o_s, o_r,
 ):
     g = lax.axis_index("group")
     t = lax.axis_index("tensor")
@@ -70,14 +70,6 @@
         return pltpu.make_async_remote_copy(
             src_ref=src, dst_ref=dst, send_sem=ss, recv_sem=rs, device_id=where, device_id_type=MESH
         )
-
-    barrier = pltpu.get_barrier_semaphore()
-    greet = [at_z(o) for o in (1, -1, 2, -2, 4, -4, 8)]
-    greet += [at_plane((p + k) % 4) for k in (1, 2, 3)]
-    greet += [dev((g + k) % NG, t) for k in range(1, NG)]
-    greet += [dev((g + k) % NG, z * 4 + across) for k in range(1, NG)]
-    for where in greet:
-        pl.semaphore_signal(barrier, inc=1, device_id=where, device_id_type=MESH)
 
     def quarter_cols(q):
         return pl.ds(pl.multiple_of((2 * (q % 2) + q // 2) * QUARTER, QUARTER), QUARTER)
@@ -101,6 +93,14 @@
     for load in load_state:
         load.start()
 
+    barrier = pltpu.get_barrier_semaphore()
+    greet = [at_z(o) for o in (1, -1, 2, -2, 4, -4, 8)]
+    greet += [at_plane((p + k) % 4) for k in (1, 2, 3)]
+    greet += [dev((g + k) % NG, t) for k in range(1, NG)]
+    greet += [dev((g + k) % NG, z * 4 + across) for k in range(1, NG)]
+    for where in greet:
+        pl.semaphore_signal(barrier, inc=1, device_id=where, device_id_type=MESH)
+
     load_hidden.wait()
     load_gain.wait()
     values = hidden_v[0].astype(F32)
@@ -172,31 +172,31 @@
     def cot_out(w):
         return copy(cot, cots.at[p], cot_s.at[w], cot_r.at[p], at_plane(lane_of[w]))
 
+    @pl.when((g == 0) & (p == 0))
+    def _():
+        n0[z, 0] = nmine[0, :, 0:WIDTHS[0]]
+
+    nbuf[z, xh] = nmine[xh]
+
+    @pl.when(any_lane)
+    def _():
+        for k in range(NZ):
+            n0[k, 1 - xl] = jnp.zeros((CHIP_ROWS, WIDTHS[0]), BF16)
+
+    @pl.when(is_lane[1])
+    def _():
+        for k in range(NZ):
+            n0[k, xl, :, WIDTHS[1]:WIDTHS[0]] = jnp.zeros((CHIP_ROWS, WIDTHS[0] - WIDTHS[1]), BF16)
+
+    copy(nmine.at[xh], nbuf.at[z, 1 - xh], x_s, x_r, partner).wait_recv()
+    for d in range(2):
+        ring(d, 0, 1).start()
+
     for w in range(2):
         pl.when(p != lane_of[w])(cot_out(w).start)
     for i in range(1, 4):
         for k in range(3):
             st(k, i).start()
-
-    @pl.when((g == 0) & (p == 0))
-    def _():
-        n0[z, 0] = nmine[0, :, 0:WIDTHS[0]]
-
-    nbuf[z, xh] = nmine[xh]
-
-    @pl.when(any_lane)
-    def _():
-        for k in range(NZ):
-            n0[k, 1 - xl] = jnp.zeros((CHIP_ROWS, WIDTHS[0]), BF16)
-
-    @pl.when(is_lane[1])
-    def _():
-        for k in range(NZ):
-            n0[k, xl, :, WIDTHS[1]:WIDTHS[0]] = jnp.zeros((CHIP_ROWS, WIDTHS[0] - WIDTHS[1]), BF16)
-
-    copy(nmine.at[xh], nbuf.at[z, 1 - xh], x_s, x_r, partner).wait_recv()
-    for d in range(2):
-        ring(d, 0, 1).start()
 
     def ring_step(step):
         for chunk in range(2):
@@ -324,7 +324,7 @@
     for k, value in enumerate((w_new, m, v)):
         for q in range(4):
             newstate[k, q] = value[2 * q:2 * q + 2]
-    results = (new_master, new_first, new_second)
+    results = [new_state.at[k] for k in range(3)]
 
     def back(k, i):
         other = (p + i) % 4
@@ -342,8 +342,6 @@
 
     ring_step(4)
     ring_step(5)
-    ring_step(6)
-    ring_step(7)
 
     expand = jnp.where(
         lax.broadcasted_iota(jnp.int32, (ROWS // PAGE, ROWS), 1) // PAGE
@@ -355,37 +353,41 @@
     marks = jnp.broadcast_to(stale_v[...].astype(F32), (8, ROWS // PAGE)).astype(BF16)
     mask = jnp.dot(marks, expand, preferred_element_type=F32)[0:1]
 
+    ring_step(6)
+
     for k in range(1, NG):
         other = (g + k) % NG
         copy(wtile, wbuf.at[other], w2_s.at[k - 1], w2_r.at[other], dev(other, t)).wait_recv()
     reorder = select_matrix((PLANE_CH, PLANE_CH), lambda c: ((c % 32) // 2) * 8 + (c // 32) * 2 + c % 2)
-    weights = jnp.dot(
+    wmat[...] = jnp.dot(
         reorder, wbuf[...].astype(F32).reshape(PLANE_CH, QUARTER).astype(BF16), preferred_element_type=F32
     ).astype(BF16)
 
-    ring_step(8)
-
-    for k in range(6):
-        rows = slice(256 * k, 256 * (k + 1))
-        block = nbuf[...].reshape(ROWS, QUARTER)[rows]
-        obuf[:, :, :, rows] = lax.dot_general(
-            weights, block, (((1,), (1,)), ((), ())), preferred_element_type=F32
-        ).reshape(2, 2, 32, 256)
-
-    def o1_copy(k):
-        return copy(obuf.at[k, 1 - co], o1.at[k], o1_s.at[k], o1_r.at[k], sibling)
-
-    o1_copy(1 - xh).start()
-    o1_copy(xh).start()
-    o1_copy(1 - xh).wait_recv()
-    o2send[...] = (obuf[1 - xh, co] + o1[1 - xh]).astype(BF16)
-    o2_out = copy(o2send, o2, o2_s, o2_r, partner)
-    o2_out.start()
-    o1_copy(xh).wait_recv()
-    osum[...] = obuf[xh, co] + o1[xh]
-    o2_out.wait_recv()
-    result = (osum[...] + o2[...].astype(F32)).astype(BF16)
-    cache[0] = jnp.where(mask > 0.5, result, old_v[0])
+    def o_copy(slot, i):
+        other = (p + i) % 4
+        return copy(opart.at[slot, other], orecv.at[p, slot], o_s.at[i - 1, slot], o_r.at[p, slot], at_plane(other))
+
+    def product(offset):
+        slot = (z + offset + NZ) % NZ
+        out = lax.dot_general(
+            wmat[...], nbuf[slot].reshape(2 * CHIP_ROWS, QUARTER), (((1,), (1,)), ((), ())), preferred_element_type=F32
+        ).reshape(4, 32, 2 * CHIP_ROWS)
+        oall[slot] = out
+        opart[slot] = out.astype(BF16)
+        for i in range(1, 4):
+            o_copy(slot, i).start()
+
+    def products(first_offset, count):
+        def body(i, carry):
+            product(first_offset + i)
+            return carry
+
+        lax.fori_loop(0, count, body, 0)
+
+    products(-3, 7)
+    ring_step(7)
+    products(-7, 4)
+    products(4, 4)
 
     for k in range(3):
         keep[k].wait()
@@ -401,11 +403,6 @@
     x_out.wait_send()
     for w in range(2):
         pl.when(p != lane_of[w])(cot_out(w).wait_send)
-    for step in range(8):
-        for chunk in range(2):
-            for d in range(2):
-                if step < steps(d, chunk):
-                    ring(d, step, chunk).wait_send()
     for j in range(4):
         for w in range(2):
             pl.when(l1_cond(j, w))(l1(j, w).wait_send)
@@ -420,16 +417,40 @@
                 pl.when((g != k) | (p != holder))(l5(k, w).wait_send)
     for k in range(1, NG):
         copy(wtile, wbuf.at[g], w2_s.at[k - 1], w2_r.at[g], dev((g + k) % NG, t)).wait_send()
-    o1_copy(1 - xh).wait_send()
-    o1_copy(xh).wait_send()
-    o2_out.wait_send()
+
+    def ring_sent(step):
+        for chunk in range(2):
+            for d in range(2):
+                if step < steps(d, chunk):
+                    ring(d, step, chunk).wait_send()
+
+    for step in range(7):
+        ring_sent(step)
+
+    ring_step(8)
+    product(8)
+    ring_sent(7)
+
+    for slot in range(NZ):
+        part = oall[slot, p]
+        for i in range(1, 4):
+            other = (p + i) % 4
+            copy(
+                opart.at[slot, p], orecv.at[other, slot], o_s.at[i - 1, slot], o_r.at[other, slot], at_plane(other)
+            ).wait_recv()
+            part = part + orecv[other, slot].astype(F32)
+        joined[:, slot * 2 * CHIP_ROWS:(slot + 1) * 2 * CHIP_ROWS] = part
+    cache[0] = jnp.where(mask > 0.5, joined[...].astype(BF16), old_v[0])
+
+    for slot in range(NZ):
+        for i in range(1, 4):
+            o_copy(slot, i).wait_send()
 
 
 def local(hidden, norm_gain, cotangent, master, first_moment, second_moment, old_cache, stale_pages):
     dma = pltpu.SemaphoreType.DMA
     vmem = pl.BlockSpec(memory_space=pltpu.VMEM)
     hbm = pl.BlockSpec(memory_space=pl.ANY)
-    state = jax.ShapeDtypeStruct((2, D), F32)
     scratch = [
         pltpu.VMEM((1, DEV_ROWS, D), BF16),
         pltpu.VMEM((1, D), F32),
@@ -448,22 +469,22 @@
         pltpu.VMEM((3, 4, 2, QUARTER), F32),
         pltpu.VMEM((8, QUARTER), BF16),
         pltpu.VMEM((NG, 8, QUARTER), BF16),
-        pltpu.VMEM((2, 2, 32, ROWS), F32),
-        pltpu.VMEM((2, 32, ROWS), F32),
+        pltpu.VMEM((PLANE_CH, QUARTER), BF16),
+        pltpu.VMEM((NZ, 4, 32, 2 * CHIP_ROWS), F32),
+        pltpu.VMEM((NZ, 4, 32, 2 * CHIP_ROWS), BF16),
+        pltpu.VMEM((4, NZ, 32, 2 * CHIP_ROWS), BF16),
         pltpu.VMEM((32, ROWS), F32),
-        pltpu.VMEM((32, ROWS), BF16),
-        pltpu.VMEM((32, ROWS), BF16),
         dma((4,)), dma, dma, dma, dma, dma((2, 8, 2)), dma((2, 8, 2)), dma((2,)), dma((4,)),
         dma((3, 3)), dma((3, 4)), dma((4, 2)), dma,
         dma((3,)), dma((3,)), dma((4,)), dma((4,)),
         dma((NG,)), dma((2, 2, 2)), dma((3, 3)), dma((3, 4)), dma((NG - 1,)), dma((NG,)),
-        dma((2,)), dma((2,)), dma, dma,
+        dma((3, NZ)), dma((4, NZ)),
     ]
-    return pl.pallas_call(
+    new_state, cache = pl.pallas_call(
         kernel,
-        out_shape=(state, state, state, jax.ShapeDtypeStruct(old_cache.shape, BF16)),
+        out_shape=(jax.ShapeDtypeStruct((3, 2, D), F32), jax.ShapeDtypeStruct(old_cache.shape, BF16)),
         in_specs=[hbm] * 8,
-        out_specs=(vmem,) * 4,
+        out_specs=(vmem,) * 2,
         scratch_shapes=scratch,
         compiler_params=pltpu.CompilerParams(
             collective_id=0, has_side_effects=True, vmem_limit_bytes=56 * 1024 * 1024
@@ -472,6 +493,7 @@
     )(
         hidden, norm_gain.reshape(1, D), cotangent, master, first_moment, second_moment, old_cache, stale_pages
     )
+    return new_state[0], new_state[1], new_state[2], cache
 
 
 def solution(mesh):

time: 92.5 us -> 89.8 us (0.971)
  Pallas kernels: 88.3 us -> 86.8 us
  local copies, waits for them, and re-layouts: 3.3 us -> 2.14 us
    unnamed x10 -> x3, local copies, waits for them, and re-layouts: 3.3 us -> 0.64 us
    squeeze x0 -> x1, local copies, waits for them, and re-layouts: none -> 1.5 us  [local(): return (new_state[0], new_state[1], new_state[2], cache)]
    pallas_call x1, Pallas kernels: 88.3 us -> 86.8 us  [local(): pl.pallas_call(kernel, out_shape=(jax.ShapeDtypeStruct((3, 2, D), F32), j...]
where the time goes in v3:
time: 89.8 us; the launch traced here: 89.6 us
  Pallas kernels  86.8 us (97%)
  local copies, waits for them, and re-layouts  2.14 us (2%)
    pallas_call x1, Pallas kernels, local(): pl.pallas_call(kernel, out_shape=(jax.ShapeDtypeStruct((3, 2, D), F32), j...  86.8 us

profile of v3, /device:TPU:1, one launch (start us, length us, event | category | flops | bytes accessed | tf_op | source)
XLA Modules:
  0.0 89.6 jit_solution(1497777485062603514)
XLA Ops:
  0.6 86.8 %shard_map.111 = (f32[3,2,5120]{2,1,0:T(2,128)}, bf16[1,32,1536]{2,1,0:T(8,128)(2,1)}) custom-call(bf16[1,24,5120]{2,1,0:T(8,128)(2,1)} %hidden.1, f32[1,5120]{1,0:T(1,128)} %bitcast.7, bf16[32,1536]{1,0:T(8,128)(2,1)} %cot.1, f32[2,5120]{1,0:T(2,128)} %master.1, f32[2,5120]{1,0:T(2,128)} %first.1, f32[2,5120]{1,0:T(2,128)} %second.1, ...), custom_call_target="tpu_custom_call" | custom-call | flops 800000000 | bytes 2000000 | tf_op jit(solution)/shard_map/pallas_call | solution.py:483
  87.4 0.0 copy-start
  87.4 1.5 %slice_bitcast_fusion = (f32[2,5120]{1,0:T(2,128)}, f32[2,5120]{1,0:T(2,128)}, f32[2,5120]{1,0:T(2,128)}) fusion(f32[3,2,5120]{2,1,0:T(2,128)} %get-tuple-element.6), kind=kLoop, calls=%fused_computation | loop fusion | bytes 245760 | tf_op jit(solution)/shard_map/squeeze | solution.py:496
  88.9 0.0 copy-done
  88.9 0.6 copy.13
Async XLA Ops:
  87.4 1.5 %copy-start = (bf16[1,32,1536]{2,1,0:T(8,128)(2,1)S(1)}, bf16[1,32,1536]{2,1,0:T(8,128)(2,1)}, u32[]{:S(2)}) copy-start(bf16[1,32,1536]{2,1,0:T(8,128)(2,1)} %get-tuple-element.18) | copy-start | bytes 294916

commit v4 on v3

--- a/solution.py
+++ b/solution.py
@@ -41,7 +41,7 @@
     new_state, cache,
     hidden_v, gain_v, old_v, stale_v, nsend, ncore, nmine, nbuf, n0, cots, cotp, gsend, grecv, state, newstate,
     wtile, wbuf, wmat, oall, opart, orecv, joined,
-    in_s, core_s, core_r, x_s, x_r, ring_s, ring_r, cot_s, cot_r, st_s, st_r, l1_s, l1_r, l2_s, l2_r, l3_s, l3_r,
+    in_s, core_s, core_r, x_s, x_r, begin_s, begin_r, ring_s, ring_r, cot_s, cot_r, st_s, st_r, l1_s, l1_r, l2_s, l2_r, l3_s, l3_r,
     l5_s, l5_r, back_s, back_r, w2_s, w2_r, o_s, o_r,
 ):
     g = lax.axis_index("group")
@@ -160,8 +160,15 @@
     for j in range(4):
         for w in range(2):
             pl.when(l1_cond(j, w))(l1(j, w).start)
-    x_out = copy(nmine.at[1 - xh], nbuf.at[z, xh], x_s, x_r, partner)
-    x_out.start()
+    pieces = (slice(0, 32), slice(32, CHIP_ROWS))
+
+    def x_out(h):
+        return copy(
+            nmine.at[1 - xh, pieces[h]], nbuf.at[z, xh, pieces[h]], x_s.at[h], x_r.at[h], partner
+        )
+
+    for h in range(2):
+        x_out(h).start()
     for d in range(2):
         ring(d, 0, 0).start()
 
@@ -188,9 +195,17 @@
         for k in range(NZ):
             n0[k, xl, :, WIDTHS[1]:WIDTHS[0]] = jnp.zeros((CHIP_ROWS, WIDTHS[0] - WIDTHS[1]), BF16)
 
-    copy(nmine.at[xh], nbuf.at[z, 1 - xh], x_s, x_r, partner).wait_recv()
-    for d in range(2):
-        ring(d, 0, 1).start()
+    def begin(d, h, arriving):
+        sign = 1 if d == 0 else -1
+        slot = (z - sign + NZ) % NZ if arriving else z
+        ref = nbuf.at[slot, 1 - xh, pieces[h]]
+        return copy(ref, ref, begin_s.at[d, h], begin_r.at[d, h], at_z(-sign if arriving else sign))
+
+    for h in range(2):
+        ref = nbuf.at[z, 1 - xh, pieces[h]]
+        copy(ref, ref, x_s.at[h], x_r.at[h], partner).wait_recv()
+        for d in range(2):
+            begin(d, h, False).start()
 
     for w in range(2):
         pl.when(p != lane_of[w])(cot_out(w).start)
@@ -201,7 +216,10 @@
     def ring_step(step):
         for chunk in range(2):
             for d in range(2):
-                if step - 1 < steps(d, chunk):
+                if step == 1 and chunk == 1:
+                    for h in range(2):
+                        begin(d, h, True).wait_recv()
+                elif step - 1 < steps(d, chunk):
                     ring_in(d, step - 1, chunk).wait_recv()
                 if step < steps(d, chunk):
                     ring(d, step, chunk).start()
@@ -384,10 +402,30 @@
 
         lax.fori_loop(0, count, body, 0)
 
-    products(-3, 7)
+    def collect(offset):
+        slot = (z + offset + NZ) % NZ
+        part = oall[slot, p]
+        for i in range(1, 4):
+            other = (p + i) % 4
+            copy(
+                opart.at[slot, p], orecv.at[other, slot], o_s.at[i - 1, slot], o_r.at[other, slot], at_plane(other)
+            ).wait_recv()
+            part = part + orecv[other, slot].astype(F32)
+        oall[slot, p] = part
+        for i in range(1, 4):
+            o_copy(slot, i).wait_send()
+
+    def collect_all(first_offset, count):
+        def body(i, carry):
+            collect(first_offset + i)
+            return carry
+
+        lax.fori_loop(0, count, body, 0)
+
+    products(-5, 11)
     ring_step(7)
-    products(-7, 4)
-    products(4, 4)
+    products(-7, 2)
+    products(6, 2)
 
     for k in range(3):
         keep[k].wait()
@@ -400,7 +438,8 @@
             back(k, i).wait_send()
             st(k, i).wait_send()
     core_out.wait_send()
-    x_out.wait_send()
+    for h in range(2):
+        x_out(h).wait_send()
     for w in range(2):
         pl.when(p != lane_of[w])(cot_out(w).wait_send)
     for j in range(4):
@@ -421,30 +460,25 @@
     def ring_sent(step):
         for chunk in range(2):
             for d in range(2):
-                if step < steps(d, chunk):
+                if step == 0 and chunk == 1:
+                    for h in range(2):
+                        begin(d, h, False).wait_send()
+                elif step < steps(d, chunk):
                     ring(d, step, chunk).wait_send()
 
     for step in range(7):
         ring_sent(step)
+
+    collect_all(-5, 11)
 
     ring_step(8)
     product(8)
     ring_sent(7)
-
+    collect_all(-7, 2)
+    collect_all(6, 3)
     for slot in range(NZ):
-        part = oall[slot, p]
-        for i in range(1, 4):
-            other = (p + i) % 4
-            copy(
-                opart.at[slot, p], orecv.at[other, slot], o_s.at[i - 1, slot], o_r.at[other, slot], at_plane(other)
-            ).wait_recv()
-            part = part + orecv[other, slot].astype(F32)
-        joined[:, slot * 2 * CHIP_ROWS:(slot + 1) * 2 * CHIP_ROWS] = part
+        joined[:, slot * 2 * CHIP_ROWS:(slot + 1) * 2 * CHIP_ROWS] = oall[slot, p]
     cache[0] = jnp.where(mask > 0.5, joined[...].astype(BF16), old_v[0])
-
-    for slot in range(NZ):
-        for i in range(1, 4):
-            o_copy(slot, i).wait_send()
 
 
 def local(hidden, norm_gain, cotangent, master, first_moment, second_moment, old_cache, stale_pages):
@@ -474,7 +508,7 @@
         pltpu.VMEM((NZ, 4, 32, 2 * CHIP_ROWS), BF16),
         pltpu.VMEM((4, NZ, 32, 2 * CHIP_ROWS), BF16),
         pltpu.VMEM((32, ROWS), F32),
-        dma((4,)), dma, dma, dma, dma, dma((2, 8, 2)), dma((2, 8, 2)), dma((2,)), dma((4,)),
+        dma((4,)), dma, dma, dma((2,)), dma((2,)), dma((2, 2)), dma((2, 2)), dma((2, 8, 2)), dma((2, 8, 2)), dma((2,)), dma((4,)),
         dma((3, 3)), dma((3, 4)), dma((4, 2)), dma,
         dma((3,)), dma((3,)), dma((4,)), dma((4,)),
         dma((NG,)), dma((2, 2, 2)), dma((3, 3)), dma((3, 4)), dma((NG - 1,)), dma((NG,)),

time: 89.8 us -> 88.8 us (0.989)
  Pallas kernels: 86.8 us -> 85.8 us
    pallas_call x1, Pallas kernels: 86.8 us -> 85.8 us  [local(): pl.pallas_call(kernel, out_shape=(jax.ShapeDtypeStruct((3, 2, D), F32), j...]
where the time goes in v4:
time: 88.8 us; the launch traced here: 88.6 us
  Pallas kernels  85.8 us (97%)
  local copies, waits for them, and re-layouts  2.14 us (2%)
    pallas_call x1, Pallas kernels, local(): pl.pallas_call(kernel, out_shape=(jax.ShapeDtypeStruct((3, 2, D), F32), j...  85.8 us

profile of v4, /device:TPU:1, one launch (start us, length us, event | category | flops | bytes accessed | tf_op | source)
XLA Modules:
  0.0 88.6 jit_solution(4233729175384942827)
XLA Ops:
  0.6 85.8 %shard_map.111 = (f32[3,2,5120]{2,1,0:T(2,128)}, bf16[1,32,1536]{2,1,0:T(8,128)(2,1)}) custom-call(bf16[1,24,5120]{2,1,0:T(8,128)(2,1)} %hidden.1, f32[1,5120]{1,0:T(1,128)} %bitcast.7, bf16[32,1536]{1,0:T(8,128)(2,1)} %cot.1, f32[2,5120]{1,0:T(2,128)} %master.1, f32[2,5120]{1,0:T(2,128)} %first.1, f32[2,5120]{1,0:T(2,128)} %second.1, ...), custom_call_target="tpu_custom_call" | custom-call | flops 800000000 | bytes 2000000 | tf_op jit(solution)/shard_map/pallas_call | solution.py:517
  86.5 0.0 copy-start
  86.5 1.5 %slice_bitcast_fusion = (f32[2,5120]{1,0:T(2,128)}, f32[2,5120]{1,0:T(2,128)}, f32[2,5120]{1,0:T(2,128)}) fusion(f32[3,2,5120]{2,1,0:T(2,128)} %get-tuple-element.6), kind=kLoop, calls=%fused_computation | loop fusion | bytes 245760 | tf_op jit(solution)/shard_map/squeeze | solution.py:530
  88.0 0.0 copy-done
  88.0 0.6 copy.13
Async XLA Ops:
  86.5 1.5 %copy-start = (bf16[1,32,1536]{2,1,0:T(8,128)(2,1)S(1)}, bf16[1,32,1536]{2,1,0:T(8,128)(2,1)}, u32[]{:S(2)}) copy-start(bf16[1,32,1536]{2,1,0:T(8,128)(2,1)} %get-tuple-element.18) | copy-start | bytes 294916
